TPU v7x, 256 devices: a whole 4x4x8 slice. The times are simulated.
256 devices in a mesh: dom: 16 (over x, y), fsdp: 16 (over z, core).
Axes of the slice: x: 4, y: 4, z: 8, core: 2. Of those that a mesh axis runs over, the one named last changes fastest.
Arguments:
- tokens: bfloat16 [16, 768, 4096], P('dom', 'fsdp'), may hold values from -8 to 8
- hidden_grad: bfloat16 [16, 768, 8192], P('dom', None, 'fsdp'), may hold values from -2.5 to 2.5
- gate_weight: bfloat16 [4096, 8192], P('dom', 'fsdp'), may hold values from -0.09375 to 0.09375
- up_weight: bfloat16 [4096, 8192], P('dom', 'fsdp'), may hold values from -0.09375 to 0.09375
- counts: int32 [16], replicated, may hold values from 1 to 8
Outputs:
- mix_gate: float32 [4096, 8192], P('dom', 'fsdp')
- mix_up: float32 [4096, 8192], P('dom', 'fsdp')
- alpha: float32 [16], replicated
All inputs are finite; a program needn't handle non-finite values.
Results may differ from a plain program's by a relative error of at most 0.0034.
Values may be sent and summed in bfloat16 or wider, within the bound.
A program may use at most 128 MiB of HBM per device.

v0:
```python
import jax
import jax.numpy as jnp
from jax import lax
from jax.sharding import PartitionSpec as P

STEP_SIZE = 4.0
EPS = 1e-06


def domain_weights(gram, counts):
    prior = counts.astype(jnp.float32) / jnp.sum(counts.astype(jnp.float32))
    toward = jnp.dot(gram, prior, precision=lax.Precision.HIGHEST)
    spread = jnp.dot(prior, toward, precision=lax.Precision.HIGHEST)
    cosine = toward / jnp.sqrt((jnp.diagonal(gram) + EPS) * (spread + EPS))
    scaled = prior * jnp.exp(STEP_SIZE * cosine)
    return scaled / jnp.sum(scaled)


def local(tokens, hidden_grad, gate_weight, up_weight, counts):
    domains = lax.axis_size("dom")
    features = lax.all_gather(tokens, "fsdp", axis=1, tiled=True)[0]
    block = gate_weight.shape[0]
    width_local = gate_weight.shape[1]
    gate_pre = jnp.dot(
        features,
        lax.all_gather(gate_weight, "dom", axis=0, tiled=True),
        preferred_element_type=jnp.float32,
    )
    up_pre = jnp.dot(
        features,
        lax.all_gather(up_weight, "dom", axis=0, tiled=True),
        preferred_element_type=jnp.float32,
    )
    upstream = hidden_grad[0].astype(jnp.float32)
    sig_gate = jax.nn.sigmoid(gate_pre)
    gate_act = (upstream * up_pre * sig_gate * (1.0 + gate_pre * (1.0 - sig_gate))).astype(
        jnp.bfloat16
    )
    up_act = (upstream * gate_pre * sig_gate).astype(jnp.bfloat16)
    contract = (((0,), (0,)), ((), ()))
    grad_gate = lax.dot_general(features, gate_act, contract, preferred_element_type=jnp.float32)
    grad_up = lax.dot_general(features, up_act, contract, preferred_element_type=jnp.float32)
    grad_gate = grad_gate.astype(jnp.bfloat16).reshape(domains, block, width_local)
    grad_up = grad_up.astype(jnp.bfloat16).reshape(domains, block, width_local)
    stack_gate, stack_up = (
        lax.all_to_all(grad_gate, "dom", split_axis=0, concat_axis=0, tiled=True),
        lax.all_to_all(grad_up, "dom", split_axis=0, concat_axis=0, tiled=True),
    )
    flat_gate = stack_gate.reshape(domains, -1)
    flat_up = stack_up.reshape(domains, -1)
    inner = (((1,), (1,)), ((), ()))
    gram_part = lax.dot_general(
        flat_gate, flat_gate, inner, preferred_element_type=jnp.float32
    ) + lax.dot_general(flat_up, flat_up, inner, preferred_element_type=jnp.float32)
    gram = lax.psum(gram_part, ("dom", "fsdp"))
    alpha = domain_weights(gram, counts)
    mix_gate = jnp.sum(alpha[:, None, None] * stack_gate.astype(jnp.float32), axis=0)
    mix_up = jnp.sum(alpha[:, None, None] * stack_up.astype(jnp.float32), axis=0)
    return (mix_gate, mix_up, alpha)


def solution(mesh):
    return jax.shard_map(
        local,
        mesh=mesh,
        in_specs=(
            P("dom", "fsdp", None),
            P("dom", None, "fsdp"),
            P("dom", "fsdp"),
            P("dom", "fsdp"),
            P(),
        ),
        out_specs=(P("dom", "fsdp"), P("dom", "fsdp"), P()),
        check_vma=False,
    )
```

profile of v0, /device:TPU:1, one launch (start us, length us, event | category | flops | bytes accessed | tf_op | source)
XLA Modules:
  0.0 428.7 jit_solution(12432295866732016043)
XLA Ops:
  7.2 0.0 all-gather.8.cloned.1.call-start
  7.2 0.7 all-gather.8.cloned.1.call-update
  7.9 0.0 all-gather.4.cloned.1.call-start
  7.9 0.7 all-gather.4.cloned.1.call-update
  8.6 0.0 all-gather.6.cloned.1.call-start
  8.7 0.7 all-gather.6.cloned.1.call-update
  9.4 0.0 copy-start.2
  9.4 61.4 %all-gather.8.cloned.1.call-done = bf16[4096,512]{1,0:T(8,128)(2,1)} async-done(((bf16[256,512]{1,0:T(8,128)(2,1)}), bf16[4096,512]{1,0:T(8,128)(2,1)}) %all-gather.8.cloned.1.call-update) | async-done | bytes 4194320 | tf_op jit(solution)/shard_map/all_gather | solution.py:26
  70.8 48.1 %all-gather.4.cloned.1.call-done = bf16[1,768,4096]{2,1,0:T(8,128)(2,1)} async-done(((bf16[1,48,4096]{2,1,0:T(8,128)(2,1)}), bf16[1,768,4096]{2,1,0:T(8,128)(2,1)}) %all-gather.4.cloned.1.call-update) | async-done | bytes 6291472 | tf_op jit(solution)/shard_map/all_gather | solution.py:21
  118.9 6.7 %fusion.4 = f32[768,512]{1,0:T(8,128)S(1)} fusion(bf16[4096,512]{1,0:T(8,128)(2,1)} %all-gather.8.cloned.1.call-done, bf16[1,768,4096]{2,1,0:T(8,128)(2,1)} %all-gather.4.cloned.1.call-done), kind=kOutput, calls=%fused_computation.7 | convolution fusion | flops 3221225472 | bytes 12058624 | tf_op jit(solution)/shard_map/dot_general | solution.py:24
  125.6 50.5 %all-gather.6.cloned.1.call-done = bf16[4096,512]{1,0:T(8,128)(2,1)} async-done(((bf16[256,512]{1,0:T(8,128)(2,1)}), bf16[4096,512]{1,0:T(8,128)(2,1)}) %all-gather.6.cloned.1.call-update) | async-done | bytes 4194320 | tf_op jit(solution)/shard_map/all_gather | solution.py:31
  176.1 0.0 copy-done.2
  176.1 14.9 %fusion.17 = bf16[4096,512]{0,1:T(8,128)(2,1)} fusion(bf16[1,768,4096]{2,1,0:T(8,128)(2,1)} %all-gather.4.cloned.1.call-done, f32[768,512]{1,0:T(8,128)S(1)} %fusion.4, bf16[4096,512]{1,0:T(8,128)(2,1)} %all-gather.6.cloned.1.call-done, bf16[1,768,512]{2,1,0:T(8,128)(2,1)S(1)} %copy-done.2), kind=kOutput, calls=%fused_computation.14 | convolution fusion | flops 6448873472 | bytes 17039360 | tf_op jit(solution)/shard_map/dot_general | solution.py:41
  191.0 6.5 %copy.20 = bf16[4096,512]{1,0:T(8,128)(2,1)} copy(bf16[4096,512]{0,1:T(8,128)(2,1)} %fusion.17) | data formatting | bytes 8388608 | tf_op jit(solution)/shard_map/reshape | solution.py:43
  197.4 5.0 %all-to-all-start = ((bf16[16,256,512]{2,1,0:T(8,128)(2,1)}), bf16[16,256,512]{2,1,0:T(8,128)(2,1)}, u32[]{:S(2)}, u32[]{:S(2)}) async-start(bf16[16,256,512]{2,1,0:T(8,128)(2,1)} %bitcast.56), calls=%async_computation | async-start | bytes 8388608 | tf_op jit(solution)/shard_map/all_to_all | solution.py:46
  202.5 8.0 %fusion.14 = bf16[4096,512]{0,1:T(8,128)(2,1)} fusion(bf16[1,768,4096]{2,1,0:T(8,128)(2,1)} %all-gather.4.cloned.1.call-done, f32[768,512]{1,0:T(8,128)S(1)} %fusion.4, bf16[1,768,512]{2,1,0:T(8,128)(2,1)S(1)} %copy-done.2), kind=kOutput, calls=%fused_computation.13 | convolution fusion | flops 3226075136 | bytes 12845056 | tf_op jit(solution)/shard_map/dot_general | solution.py:42
  210.5 6.5 %copy.15 = bf16[4096,512]{1,0:T(8,128)(2,1)} copy(bf16[4096,512]{0,1:T(8,128)(2,1)} %fusion.14) | data formatting | bytes 8388608 | tf_op jit(solution)/shard_map/convert_element_type | solution.py:44
  216.9 47.0 %all-to-all-done = bf16[16,256,512]{2,1,0:T(8,128)(2,1)} async-done(((bf16[16,256,512]{2,1,0:T(8,128)(2,1)}), bf16[16,256,512]{2,1,0:T(8,128)(2,1)}, u32[]{:S(2)}, u32[]{:S(2)}) %all-to-all-start) | async-done | bytes 4194336 | tf_op jit(solution)/shard_map/all_to_all | solution.py:46
  264.0 10.1 %all-to-all-start.1 = ((bf16[16,256,512]{2,1,0:T(8,128)(2,1)}), bf16[16,256,512]{2,1,0:T(8,128)(2,1)}, u32[]{:S(2)}, u32[]{:S(2)}) async-start(bf16[16,256,512]{2,1,0:T(8,128)(2,1)} %bitcast.55), calls=%async_computation.1 | async-start | bytes 8388608 | tf_op jit(solution)/shard_map/all_to_all | solution.py:47
  274.1 0.0 copy-done.1
  274.1 0.6 convert_reduce_fusion
  274.7 12.2 %fusion.33 = f32[16,16]{1,0:T(8,128)S(1)} fusion(bf16[16,256,512]{2,1,0:T(8,128)(2,1)} %all-to-all-done), kind=kOutput, calls=%fused_computation.27 | convolution fusion | flops 67108864 | bytes 4195328 | tf_op jit(solution)/shard_map/dot_general | solution.py:52
  286.9 36.0 %all-to-all-done.1 = bf16[16,256,512]{2,1,0:T(8,128)(2,1)} async-done(((bf16[16,256,512]{2,1,0:T(8,128)(2,1)}), bf16[16,256,512]{2,1,0:T(8,128)(2,1)}, u32[]{:S(2)}, u32[]{:S(2)}) %all-to-all-start.1) | async-done | bytes 4194336 | tf_op jit(solution)/shard_map/all_to_all | solution.py:47
  322.9 8.4 %fusion.39 = f32[16,16]{1,0:T(8,128)S(1)} fusion(f32[16,16]{1,0:T(8,128)S(1)} %fusion.33, bf16[16,256,512]{2,1,0:T(8,128)(2,1)} %all-to-all-done.1), kind=kOutput, calls=%fused_computation.29 | convolution fusion | flops 67109120 | bytes 4196352 | tf_op jit(solution)/shard_map/dot_general | solution.py:54
  331.3 80.0 %psum.7 = f32[16,16]{1,0:T(8,128)S(1)} all-reduce(f32[16,16]{1,0:T(8,128)S(1)} %fusion.39), channel_id=1, replica_groups=mesh['dom'=16,'fsdp'=16] {'dom','fsdp'}, use_global_device_ids=true, to_apply=%region_1.0 | all-reduce | flops 256 | bytes 2048 | tf_op jit(solution)/shard_map/psum | solution.py:55
  411.3 0.7 gather_fusion
  412.0 1.4 multiply_reduce_fusion.2
  414.0 1.3 fusion.50
  415.3 0.6 broadcast_divide_fusion
  416.0 0.0 copy-start
  416.0 6.2 %multiply_reduce_fusion = (f32[256,512]{1,0:T(8,128)}, f32[256,512]{1,0:T(8,128)}) fusion(bf16[16,256,512]{2,1,0:T(8,128)(2,1)} %all-to-all-done.1, f32[16]{0:T(128)S(1)} %broadcast_divide_fusion, bf16[16,256,512]{2,1,0:T(8,128)(2,1)} %all-to-all-done), kind=kLoop, calls=%fused_computation.1 | loop fusion | flops 12320768 | bytes 9437248 | tf_op jit(solution)/shard_map/reduce_sum | solution.py:58
  422.2 0.0 copy-done
  (2 shorter events, 0.0 us)
Async XLA Ops:
  7.2 63.6 %all-gather.8.cloned.1.call-start = ((), (), s32[]{:S(2)}) async-start(), calls=%async_computation.4 | async-start | bytes 4456448 | tf_op jit(solution)/shard_map/all_gather | solution.py:26
  7.9 111.0 %all-gather.4.cloned.1.call-start = ((), (), s32[]{:S(2)}) async-start(), calls=%async_computation.2 | async-start | bytes 6684672 | tf_op jit(solution)/shard_map/all_gather | solution.py:21
  8.6 167.4 %all-gather.6.cloned.1.call-start = ((), (), s32[]{:S(2)}) async-start(), calls=%async_computation.3 | async-start | bytes 4456448 | tf_op jit(solution)/shard_map/all_gather | solution.py:31
  9.4 166.7 %copy-start.2 = (bf16[1,768,512]{2,1,0:T(8,128)(2,1)S(1)}, bf16[1,768,512]{2,1,0:T(8,128)(2,1)}, u32[]{:S(2)}) copy-start(bf16[1,768,512]{2,1,0:T(8,128)(2,1)} %param.6) | copy-start | bytes 2359300
  197.4 66.5 %all-to-all-start = ((bf16[16,256,512]{2,1,0:T(8,128)(2,1)}), bf16[16,256,512]{2,1,0:T(8,128)(2,1)}, u32[]{:S(2)}, u32[]{:S(2)}) async-start(bf16[16,256,512]{2,1,0:T(8,128)(2,1)} %bitcast.56), calls=%async_computation | async-start | bytes 8388608 | tf_op jit(solution)/shard_map/all_to_all | solution.py:46
  264.0 10.1 %copy-start.1 = (s32[16]{0:T(128)S(1)}, s32[16]{0:T(128)}, u32[]{:S(2)}) copy-start(s32[16]{0:T(128)} %param.9) | copy-start | bytes 196
  264.0 58.9 %all-to-all-start.1 = ((bf16[16,256,512]{2,1,0:T(8,128)(2,1)}), bf16[16,256,512]{2,1,0:T(8,128)(2,1)}, u32[]{:S(2)}, u32[]{:S(2)}) async-start(bf16[16,256,512]{2,1,0:T(8,128)(2,1)} %bitcast.55), calls=%async_computation.1 | async-start | bytes 8388608 | tf_op jit(solution)/shard_map/all_to_all | solution.py:47
  416.0 6.3 %copy-start = (f32[16]{0:T(128)}, f32[16]{0:T(128)S(1)}, u32[]{:S(2)}) copy-start(f32[16]{0:T(128)S(1)} %broadcast_divide_fusion) | copy-start | bytes 196
Sparse Core Ops, SparseCore 0:
  10.4 60.3 all-gather.7
  72.6 46.1 all-gather.3
  121.3 54.7 all-gather.5
where the time goes:
time: 429 us
  waiting for transfers between devices  245 us (57%)
  blocking collectives  80 us (19%)
  matrix products  51.6 us (12%)
  starting transfers between devices  15.2 us (4%)
  between operations  14.5 us (3%)
  local copies, waits for them, and re-layouts  13.6 us (3%)
  other arithmetic  8.77 us (2%)
    psum x1, blocking collectives, local(): gram = lax.psum(gram_part, ('dom', 'fsdp'))  80 us
    all_gather x1, waiting for transfers between devices, local(): lax.all_gather(gate_weight, 'dom', axis=0, tiled=True)  61.4 us
    all_gather x1, waiting for transfers between devices, local(): lax.all_gather(up_weight, 'dom', axis=0, tiled=True)  50.5 us
    all_gather x1, waiting for transfers between devices, local(): features = lax.all_gather(tokens, 'fsdp', axis=1, tiled=True)[0]  48.1 us
    all_to_all x1, waiting for transfers between devices, local(): lax.all_to_all(grad_gate, 'dom', split_axis=0, concat_axis=0, tiled=True)  47 us
    all_to_all x1, waiting for transfers between devices, local(): lax.all_to_all(grad_up, 'dom', split_axis=0, concat_axis=0, tiled=True)  36 us
    dot_general x1, matrix products, local(): lax.dot_general(features, gate_act, contract, preferred_element_type=jnp....  14.9 us
    dot_general x1, matrix products, local(): lax.dot_general(flat_gate, flat_gate, inner, preferred_element_type=jnp.f...  12.2 us
  transfers between devices with their start and end apart: 5, of which 5 were waited for; matrix products, arithmetic and copies ran while one was open for 8% of the time, Pallas kernels for 0%

commit v1 on v0

v1 whole, which is shorter than its diff:
```python
import functools

import jax
import jax.numpy as jnp
from jax import lax
from jax.experimental import pallas as pl
from jax.experimental.pallas import tpu as pltpu
from jax.sharding import PartitionSpec as P

STEP_SIZE = 4.0
EPS = 1e-06
MESH = pl.DeviceIdType.MESH

SIDE = 4
N_DOM = 16
N_FSDP = 16
CHUNKS = 4
LANES = 128
ROWS = 256
TOK = 48
TOKENS = 768
D = 4096
HALF_D = D // 2


def wrap(i, n):
    return lax.rem(i + n, n)


def remote(src, dst, ss, rs, **where):
    return pltpu.make_async_remote_copy(
        src_ref=src, dst_ref=dst, send_sem=ss, recv_sem=rs, device_id=where, device_id_type=MESH
    )


def kernel(
    tok_ref, hg_ref, gw_ref, uw_ref, cnt_ref,
    og_ref, ou_ref, oa_ref,
    tokens, tokens_t, weights, grads, stack, acts, mean, scale, part, part2, ar1, ar2,
    rs_s, rs_r, sb_s, sb_r, w1_s, w1_r, w2_s, w2_r, g_s, g_r, a1_s, a1_r, a2_s, a2_r,
):
    me = lax.axis_index("dom")
    x, y = me // SIDE, lax.rem(me, SIDE)
    f = lax.axis_index("fsdp")
    z, core = f // 2, lax.rem(f, 2)
    way = 1 - 2 * core
    sibling = f + way
    onward = wrap(z + way, 8) * 2 + core

    barrier = pltpu.get_barrier_semaphore()

    @pl.loop(1, N_DOM)
    def _(k):
        pl.semaphore_signal(barrier, inc=1, device_id={"dom": lax.rem(me + k, N_DOM)}, device_id_type=MESH)
        pl.semaphore_signal(barrier, inc=1, device_id={"fsdp": lax.rem(f + k, N_FSDP)}, device_id_type=MESH)

    pl.semaphore_wait(barrier, 2 * (N_DOM - 1))

    def shard(s, c, h):
        owner = wrap(z - s * (1 - 2 * c) + 8, 8) * 2 + c
        return tokens.at[pl.ds(pl.multiple_of(owner * TOK, 16), TOK), pl.ds(h * HALF_D, HALF_D)]

    def ring(s, h):
        src = tok_ref.at[0, :, pl.ds(h * HALF_D, HALF_D)] if s == 0 else shard(s, core, h)
        return remote(src, shard(s, core, h), rs_s.at[s, h], rs_r.at[s, h], fsdp=onward)

    def side(s, h):
        src = tok_ref.at[0, :, pl.ds(h * HALF_D, HALF_D)] if s == 0 else shard(s, core, h)
        return remote(src, shard(s, core, h), sb_s.at[s, h], sb_r.at[s, h], fsdp=sibling)

    def token_step(s):
        for h in range(2):
            here = shard(s, core, h)
            remote(here, here, rs_s.at[s - 1, h], rs_r.at[s - 1, h], fsdp=onward).wait_recv()
            if s < 7:
                ring(s, h).start()
            side(s, h).start()

    def block(kind, c, bx, by, lo=0, n=ROWS):
        return weights.at[kind, c, bx, by, pl.ds(lo, n)]

    def line(kind, c, off, lo=0, n=ROWS):
        if kind == 0:
            return weights.at[kind, c, :, wrap(y + off, SIDE), pl.ds(lo, n)]
        return weights.at[kind, c, wrap(x + off, SIDE), :, pl.ds(lo, n)]

    def near(axis, off):
        if axis == 0:
            return wrap(x + off, SIDE) * SIDE + y
        return x * SIDE + wrap(y + off, SIDE)

    def first(kind, c, off, lo=0, n=ROWS):
        if kind == 0:
            return block(kind, c, wrap(x + off, SIDE), y, lo, n)
        return block(kind, c, x, wrap(y + off, SIDE), lo, n)

    HALF = ROWS // 2

    def w1(kind, c, i):
        axis, to = kind, (1, -1)[i % 2]
        if i < 2:
            src_ref = (gw_ref, uw_ref)[kind]
            src = src_ref.at[:, pl.ds(pl.multiple_of(c * LANES, LANES), LANES)]
            return remote(src, first(kind, c, 0), w1_s.at[kind, c, i], w1_r.at[kind, c, i], dom=near(axis, to))
        part_ = first(kind, c, -to, (i - 2) * HALF, HALF)
        return remote(part_, part_, w1_s.at[kind, c, i], w1_r.at[kind, c, i], dom=near(axis, to))

    def w1_got(kind, c, i):
        to = (1, -1)[i % 2]
        here = first(kind, c, -to) if i < 2 else first(kind, c, 2, (i - 2) * HALF, HALF)
        remote(here, here, w1_s.at[kind, c, i], w1_r.at[kind, c, i], dom=near(kind, to)).wait_recv()

    def w2(kind, c, i):
        axis, to = 1 - kind, (1, -1)[i % 2]
        src = line(kind, c, 0) if i < 2 else line(kind, c, -to, (i - 2) * HALF, HALF)
        return remote(src, src, w2_s.at[kind, c, i], w2_r.at[kind, c, i], dom=near(axis, to))

    def w2_got(kind, c, i):
        to = (1, -1)[i % 2]
        here = line(kind, c, -to) if i < 2 else line(kind, c, 2, (i - 2) * HALF, HALF)
        remote(here, here, w2_s.at[kind, c, i], w2_r.at[kind, c, i], dom=near(1 - kind, to)).wait_recv()

    for h in range(2):
        ring(0, h).start()

    @pl.loop(0, CHUNKS)
    def _(c):
        for kind in range(2):
            for i in range(2):
                w1(kind, c, i).start()

    for h in range(2):
        side(0, h).start()
    tokens[pl.ds(pl.multiple_of(f * TOK, 16), TOK), :] = tok_ref[0]
    for c in range(CHUNKS):
        weights[0, c, x, y] = gw_ref[:, c * LANES : (c + 1) * LANES]
        weights[1, c, x, y] = uw_ref[:, c * LANES : (c + 1) * LANES]

    counts = cnt_ref[...].astype(jnp.float32)
    prior = counts / jnp.sum(counts, axis=0, keepdims=True)

    def spread_out(column):
        for j in range(N_DOM):
            scale[j] = jnp.broadcast_to(column[j : j + 1, :], (1, 2 * LANES))

    spread_out(prior)
    part[...] = jnp.zeros_like(part)

    def stage_a(c):
        for kind in range(2):
            for i in range(2):
                w1_got(kind, c, i)
                w1(kind, c, i + 2).start()

    def stage_b(c):
        for kind in range(2):
            for i in range(2, 4):
                w1_got(kind, c, i)
            for i in range(2):
                w2(kind, c, i).start()

    def stage_c(c):
        for kind in range(2):
            for i in range(2):
                w2_got(kind, c, i)
                w2(kind, c, i + 2).start()

    def stage_d(c):
        for kind in range(2):
            for i in range(2, 4):
                w2_got(kind, c, i)

    token_step(1)
    pl.loop(0, CHUNKS)(stage_a)
    token_step(2)
    pl.loop(0, CHUNKS)(stage_b)
    token_step(3)
    token_step(4)
    stage_c(0)
    token_step(5)
    token_step(6)
    stage_c(1)
    token_step(7)
    stage_c(2)

    @pl.loop(0, 8)
    def _(s):
        for h in range(2):
            here = shard(s, 1 - core, h)
            remote(here, here, sb_s.at[s, h], sb_r.at[s, h], fsdp=sibling).wait_recv()

    @pl.loop(0, D // 256)
    def _(k):
        at = pl.ds(pl.multiple_of(k * 256, 256), 256)
        tokens_t[at, :] = tokens[:, at].T

    stage_c(3)

    def target(k):
        t = 1 + lax.rem(k + 8, N_DOM - 1)
        return wrap(x + t // SIDE, SIDE) * SIDE + wrap(y + lax.rem(t, SIDE), SIDE)

    def chunk(c):
        stage_d(c)

        @pl.loop(0, TOKENS // 256)
        def _(m):
            at = pl.ds(pl.multiple_of(m * 256, 256), 256)
            w = jnp.concatenate([weights[0, c].reshape(D, LANES), weights[1, c].reshape(D, LANES)], axis=1)
            pre = jnp.dot(tokens[at, :], w, preferred_element_type=jnp.float32)
            gate, up = pre[:, :LANES], pre[:, LANES:]
            g = hg_ref[0, at, pl.ds(pl.multiple_of(c * LANES, LANES), LANES)].astype(jnp.float32)
            s = jax.nn.sigmoid(gate)
            acts[at, :LANES] = (g * up * s * (1.0 + gate * (1.0 - s))).astype(jnp.bfloat16)
            acts[at, LANES:] = (g * gate * s).astype(jnp.bfloat16)

        def block_of(t):
            rows = pl.ds(pl.multiple_of(t * ROWS, ROWS), ROWS)
            out = jnp.dot(tokens_t[rows, :], acts[...], preferred_element_type=jnp.float32)
            return out.astype(jnp.bfloat16)

        @pl.loop(1, N_DOM)
        def _(k):
            t = target(k)
            grads[c, t] = block_of(t)
            remote(grads.at[c, t], stack.at[c, me], g_s.at[c, t], g_r.at[c, me], dom=t).start()

        stack[c, me] = block_of(me)

    pl.loop(0, CHUNKS)(chunk)

    def products(c):
        @pl.loop(1, N_DOM)
        def _(k):
            j = lax.rem(me + k, N_DOM)
            here = stack.at[c, j]
            remote(here, here, g_s.at[c, j], g_r.at[c, j], dom=j).wait_recv()

        @pl.loop(0, ROWS // 32)
        def _(r):
            at = pl.ds(pl.multiple_of(r * 32, 32), 32)
            total = scale[0] * stack[c, 0, at, :].astype(jnp.float32)
            for j in range(1, N_DOM):
                total += scale[j] * stack[c, j, at, :].astype(jnp.float32)
            mean[at, :] = total

        @pl.loop(0, N_DOM)
        def _(j):
            toward = jnp.zeros((8, 2 * LANES), jnp.float32)
            own = jnp.zeros((8, 2 * LANES), jnp.float32)
            for r in range(ROWS // 32):
                at = pl.ds(r * 32, 32)
                g = stack[c, j, at, :].astype(jnp.float32)
                toward += jnp.sum((g * mean[at, :]).reshape(4, 8, 2 * LANES), axis=0)
                own += jnp.sum((g * g).reshape(4, 8, 2 * LANES), axis=0)
            toward = jnp.sum(toward, axis=0, keepdims=True)
            own = jnp.sum(own, axis=0, keepdims=True)
            part[j] += toward[:, :LANES] + toward[:, LANES:]
            part[N_DOM + j] += own[:, :LANES] + own[:, LANES:]

    pl.loop(0, CHUNKS)(products)

    ar1[me] = part[...]

    @pl.loop(1, N_DOM)
    def _(k):
        t = lax.rem(me + k, N_DOM)
        remote(part, ar1.at[me], a1_s.at[t], a1_r.at[me], dom=t).start()

    @pl.loop(1, N_DOM)
    def _(k):
        t = lax.rem(me + k, N_DOM)
        remote(part, ar1.at[t], a1_s.at[t], a1_r.at[t], dom=t).wait_recv()

    total = ar1[0]
    for j in range(1, N_DOM):
        total += ar1[j]
    part2[...] = total
    ar2[f] = total

    @pl.loop(1, N_FSDP)
    def _(k):
        t = lax.rem(f + k, N_FSDP)
        remote(part2, ar2.at[f], a2_s.at[t], a2_r.at[f], fsdp=t).start()

    @pl.loop(1, N_FSDP)
    def _(k):
        t = lax.rem(f + k, N_FSDP)
        remote(part2, ar2.at[t], a2_s.at[t], a2_r.at[t], fsdp=t).wait_recv()

    total = ar2[0]
    for j in range(1, N_FSDP):
        total += ar2[j]
    total = jnp.sum(total.reshape(2 * N_DOM, LANES), axis=1, keepdims=True)
    toward, own = total[:N_DOM], total[N_DOM:]
    spread = jnp.sum(prior * toward, axis=0, keepdims=True)
    cosine = toward / jnp.sqrt((own + EPS) * (spread + EPS))
    scaled = prior * jnp.exp(STEP_SIZE * cosine)
    alpha = scaled / jnp.sum(scaled, axis=0, keepdims=True)
    oa_ref[...] = jnp.broadcast_to(alpha, (N_DOM, LANES))
    spread_out(alpha)

    for c in range(CHUNKS):
        cols = pl.ds(c * LANES, LANES)

        @pl.loop(0, ROWS // 32)
        def _(r):
            at = pl.ds(pl.multiple_of(r * 32, 32), 32)
            mix = scale[0] * stack[c, 0, at, :].astype(jnp.float32)
            for j in range(1, N_DOM):
                mix += scale[j] * stack[c, j, at, :].astype(jnp.float32)
            og_ref[at, cols] = mix[:, :LANES]
            ou_ref[at, cols] = mix[:, LANES:]

    for h in range(2):
        for s in range(7):
            ring(s, h).wait_send()
        for s in range(8):
            side(s, h).wait_send()

    @pl.loop(0, CHUNKS)
    def _(c):
        for kind in range(2):
            for i in range(4):
                w1(kind, c, i).wait_send()
                w2(kind, c, i).wait_send()

        @pl.loop(1, N_DOM)
        def _(k):
            t = lax.rem(me + k, N_DOM)
            remote(grads.at[c, t], stack.at[c, me], g_s.at[c, t], g_r.at[c, me], dom=t).wait_send()

    @pl.loop(1, N_DOM)
    def _(k):
        t = lax.rem(me + k, N_DOM)
        remote(part, ar1.at[me], a1_s.at[t], a1_r.at[me], dom=t).wait_send()
        t = lax.rem(f + k, N_FSDP)
        remote(part2, ar2.at[f], a2_s.at[t], a2_r.at[f], fsdp=t).wait_send()


def local(tokens, hidden_grad, gate_weight, up_weight, counts):
    vmem = pl.BlockSpec(memory_space=pltpu.VMEM)
    dma = pltpu.SemaphoreType.DMA
    bf16, f32 = jnp.bfloat16, jnp.float32
    mix_gate, mix_up, alpha = pl.pallas_call(
        kernel,
        out_shape=(
            jax.ShapeDtypeStruct((ROWS, CHUNKS * LANES), f32),
            jax.ShapeDtypeStruct((ROWS, CHUNKS * LANES), f32),
            jax.ShapeDtypeStruct((N_DOM, LANES), f32),
        ),
        in_specs=[vmem] * 5,
        out_specs=(vmem,) * 3,
        scratch_shapes=[
            pltpu.VMEM((TOKENS, D), bf16),
            pltpu.VMEM((D, TOKENS), bf16),
            pltpu.VMEM((2, CHUNKS, SIDE, SIDE, ROWS, LANES), bf16),
            pltpu.VMEM((CHUNKS, N_DOM, ROWS, 2 * LANES), bf16),
            pltpu.VMEM((CHUNKS, N_DOM, ROWS, 2 * LANES), bf16),
            pltpu.VMEM((TOKENS, 2 * LANES), bf16),
            pltpu.VMEM((ROWS, 2 * LANES), f32),
            pltpu.VMEM((N_DOM, 1, 2 * LANES), f32),
            pltpu.VMEM((2 * N_DOM, 1, LANES), f32),
            pltpu.VMEM((2 * N_DOM, 1, LANES), f32),
            pltpu.VMEM((N_DOM, 2 * N_DOM, 1, LANES), f32),
            pltpu.VMEM((N_FSDP, 2 * N_DOM, 1, LANES), f32),
            dma((7, 2)), dma((7, 2)), dma((8, 2)), dma((8, 2)),
            dma((2, CHUNKS, 4)), dma((2, CHUNKS, 4)), dma((2, CHUNKS, 4)), dma((2, CHUNKS, 4)),
            dma((CHUNKS, N_DOM)), dma((CHUNKS, N_DOM)),
            dma((N_DOM,)), dma((N_DOM,)), dma((N_FSDP,)), dma((N_FSDP,)),
        ],
        compiler_params=pltpu.CompilerParams(
            collective_id=0, has_side_effects=True, vmem_limit_bytes=56 * 2**20
        ),
        cost_estimate=pl.CostEstimate(flops=13 * 10**9, bytes_accessed=4 * 10**6, transcendentals=400000),
    )(tokens, hidden_grad, gate_weight, up_weight, counts.reshape(N_DOM, 1))
    return mix_gate, mix_up, alpha[:, 0]


def solution(mesh):
    return jax.shard_map(
        local,
        mesh=mesh,
        in_specs=(
            P("dom", "fsdp", None),
            P("dom", None, "fsdp"),
            P("dom", "fsdp"),
            P("dom", "fsdp"),
            P(),
        ),
        out_specs=(P("dom", "fsdp"), P("dom", "fsdp"), P()),
        check_vma=False,
    )
```

time: 429 us -> 192 us (0.45)
  waiting for transfers between devices: 245 us -> 0 us
  Pallas kernels: 0 us -> 186 us
  blocking collectives: 80 us -> 0 us
  matrix products: 51.6 us -> 0 us
  starting transfers between devices: 15.2 us -> 0 us
  between operations: 14.5 us -> 0.65 us
  other arithmetic: 8.77 us -> 0 us
  local copies, waits for them, and re-layouts: 13.6 us -> 5.37 us
    pallas_call x0 -> x1, Pallas kernels: none -> 186 us  [local(): pl.pallas_call(kernel, out_shape=(jax.ShapeDtypeStruct((ROWS, CHUNKS * LA...]
    all_gather x3 -> x0, waiting for transfers between devices: 160 us -> none  [the longest x1 61.4 us: local(): lax.all_gather(gate_weight, 'dom', axis=0, tiled=True)]
    all_to_all x2 -> x0, waiting for transfers between devices: 83.1 us -> none  [the longest x1 47 us: local(): lax.all_to_all(grad_gate, 'dom', split_axis=0, concat_axis=0, tiled=True)]
    psum x1 -> x0, blocking collectives: 80 us -> none  [local(): gram = lax.psum(gram_part, ('dom', 'fsdp'))]
    dot_general x6 -> x0, matrix products: 51.6 us -> none  [the longest x1 14.9 us: local(): lax.dot_general(features, gate_act, contract, preferred_element_type=jnp....]
    all_to_all x2 -> x0, starting transfers between devices: 15.1 us -> none  [the longest x1 10.1 us: local(): lax.all_to_all(grad_up, 'dom', split_axis=0, concat_axis=0, tiled=True)]
    reduce_sum x3 -> x0, other arithmetic: 8.11 us -> none  [the longest x1 6.25 us: local(): jnp.sum(alpha[:, None, None] * stack_up.astype(jnp.float32), axis=0)]
    convert_element_type x1 -> x0, local copies, waits for them, and re-layouts: 6.45 us -> none  [local(): grad_up = grad_up.astype(jnp.bfloat16).reshape(domains, block, width_local)]
  transfers between devices with their start and end apart: 5 -> 0, of which waited for: 5 -> 0; matrix products, arithmetic and copies ran while one was open for 8% -> 0% of each run, Pallas kernels for 0% -> 0%
where the time goes in v1:
time: 192 us
  Pallas kernels  186 us (97%)
  local copies, waits for them, and re-layouts  5.37 us (3%)
    pallas_call x1, Pallas kernels, local(): pl.pallas_call(kernel, out_shape=(jax.ShapeDtypeStruct((ROWS, CHUNKS * LA...  186 us

profile of v1, /device:TPU:1, one launch (start us, length us, event | category | flops | bytes accessed | tf_op | source)
XLA Modules:
  0.0 192.3 jit_solution(17593119733981610201)
XLA Ops:
  0.6 0.0 copy-start.1
  0.6 0.6 copy-done.1
  1.3 0.7 copy.9.cnt_ref
  2.0 186.3 %shard_map.76 = (f32[256,512]{1,0:T(8,128)}, f32[256,512]{1,0:T(8,128)}, f32[16,128]{1,0:T(8,128)}) custom-call(bf16[1,48,4096]{2,1,0:T(8,128)(2,1)} %tok_ref.1, bf16[1,768,512]{2,1,0:T(8,128)(2,1)} %hg_ref.1, bf16[256,512]{1,0:T(8,128)(2,1)} %gw_ref.1, bf16[256,512]{1,0:T(8,128)(2,1)} %uw_ref.1, s32[16,1]{1,0:T(8,128)} %copy.9.cnt_ref), custom_call_target="tpu_custom_call" | custom-call | flops 12999999488 | bytes 4000000 | tf_op jit(solution)/shard_map/pallas_call | solution.py:345
  188.3 1.3 slice_reduce_fusion
  189.6 0.0 copy-start
  189.6 1.9 %copy.12 = f32[256,512]{1,0:T(8,128)} copy(f32[256,512]{1,0:T(8,128)} %get-tuple-element.12) | data formatting | bytes 1048576
  191.5 0.0 copy-done
  191.5 0.8 copy.13
Async XLA Ops:
  0.6 0.7 copy-start.1
  189.6 1.9 %copy-start = (f32[256,512]{1,0:T(8,128)S(1)}, f32[256,512]{1,0:T(8,128)}, u32[]{:S(2)}) copy-start(f32[256,512]{1,0:T(8,128)} %get-tuple-element.13) | copy-start | bytes 1572868

commit v2 on v1

--- a/solution.py
+++ b/solution.py
@@ -20,7 +20,9 @@
 TOK = 48
 TOKENS = 768
 D = 4096
-HALF_D = D // 2
+PIECES = 4
+PIECE = D // PIECES
+ORDER = (10, 5, 15, 7, 13, 6, 14, 9, 11, 8, 2, 4, 1, 12, 3)
 
 
 def wrap(i, n):
@@ -36,7 +38,7 @@
 def kernel(
     tok_ref, hg_ref, gw_ref, uw_ref, cnt_ref,
     og_ref, ou_ref, oa_ref,
-    tokens, tokens_t, weights, grads, stack, acts, mean, scale, part, part2, ar1, ar2,
+    tokens, tokens_t, weights, grads, stack, acts, mean, scale, part, msg, msg2, ar1, ar2,
     rs_s, rs_r, sb_s, sb_r, w1_s, w1_r, w2_s, w2_r, g_s, g_r, a1_s, a1_r, a2_s, a2_r,
 ):
     me = lax.axis_index("dom")
@@ -58,18 +60,18 @@
 
     def shard(s, c, h):
         owner = wrap(z - s * (1 - 2 * c) + 8, 8) * 2 + c
-        return tokens.at[pl.ds(pl.multiple_of(owner * TOK, 16), TOK), pl.ds(h * HALF_D, HALF_D)]
+        return tokens.at[pl.ds(pl.multiple_of(owner * TOK, 16), TOK), pl.ds(h * PIECE, PIECE)]
 
     def ring(s, h):
-        src = tok_ref.at[0, :, pl.ds(h * HALF_D, HALF_D)] if s == 0 else shard(s, core, h)
+        src = tok_ref.at[0, :, pl.ds(h * PIECE, PIECE)] if s == 0 else shard(s, core, h)
         return remote(src, shard(s, core, h), rs_s.at[s, h], rs_r.at[s, h], fsdp=onward)
 
     def side(s, h):
-        src = tok_ref.at[0, :, pl.ds(h * HALF_D, HALF_D)] if s == 0 else shard(s, core, h)
+        src = tok_ref.at[0, :, pl.ds(h * PIECE, PIECE)] if s == 0 else shard(s, core, h)
         return remote(src, shard(s, core, h), sb_s.at[s, h], sb_r.at[s, h], fsdp=sibling)
 
     def token_step(s):
-        for h in range(2):
+        for h in range(PIECES):
             here = shard(s, core, h)
             remote(here, here, rs_s.at[s - 1, h], rs_r.at[s - 1, h], fsdp=onward).wait_recv()
             if s < 7:
@@ -120,7 +122,7 @@
         here = line(kind, c, -to) if i < 2 else line(kind, c, 2, (i - 2) * HALF, HALF)
         remote(here, here, w2_s.at[kind, c, i], w2_r.at[kind, c, i], dom=near(1 - kind, to)).wait_recv()
 
-    for h in range(2):
+    for h in range(PIECES):
         ring(0, h).start()
 
     @pl.loop(0, CHUNKS)
@@ -129,21 +131,25 @@
             for i in range(2):
                 w1(kind, c, i).start()
 
-    for h in range(2):
+    for h in range(PIECES):
         side(0, h).start()
     tokens[pl.ds(pl.multiple_of(f * TOK, 16), TOK), :] = tok_ref[0]
     for c in range(CHUNKS):
         weights[0, c, x, y] = gw_ref[:, c * LANES : (c + 1) * LANES]
         weights[1, c, x, y] = uw_ref[:, c * LANES : (c + 1) * LANES]
 
-    counts = cnt_ref[...].astype(jnp.float32)
-    prior = counts / jnp.sum(counts, axis=0, keepdims=True)
+    count = cnt_ref[0]
+    for j in range(1, N_DOM):
+        count += cnt_ref[j]
+    count = jnp.full((1, 2 * LANES), count.astype(jnp.float32))
+    for j in range(N_DOM):
+        scale[j] = jnp.full((1, 2 * LANES), cnt_ref[j].astype(jnp.float32)) / count
+    prior = scale[...].reshape(N_DOM, 2 * LANES)[:, :1]
 
     def spread_out(column):
         for j in range(N_DOM):
             scale[j] = jnp.broadcast_to(column[j : j + 1, :], (1, 2 * LANES))
 
-    spread_out(prior)
     part[...] = jnp.zeros_like(part)
 
     def stage_a(c):
@@ -175,17 +181,18 @@
     token_step(2)
     pl.loop(0, CHUNKS)(stage_b)
     token_step(3)
+    stage_c(0)
     token_step(4)
-    stage_c(0)
+    stage_c(1)
     token_step(5)
+    stage_c(2)
     token_step(6)
-    stage_c(1)
     token_step(7)
-    stage_c(2)
+    stage_c(3)
 
     @pl.loop(0, 8)
     def _(s):
-        for h in range(2):
+        for h in range(PIECES):
             here = shard(s, 1 - core, h)
             remote(here, here, sb_s.at[s, h], sb_r.at[s, h], fsdp=sibling).wait_recv()
 
@@ -194,11 +201,13 @@
         at = pl.ds(pl.multiple_of(k * 256, 256), 256)
         tokens_t[at, :] = tokens[:, at].T
 
-    stage_c(3)
-
     def target(k):
-        t = 1 + lax.rem(k + 8, N_DOM - 1)
-        return wrap(x + t // SIDE, SIDE) * SIDE + wrap(y + lax.rem(t, SIDE), SIDE)
+        t = ORDER[0]
+        for i in range(1, N_DOM - 1):
+            t = jnp.where(k == i, ORDER[i], t)
+        dx, dy = t // SIDE, lax.rem(t, SIDE)
+        dx, dy = dx + core * (dy - dx), dy + core * (dx - dy)
+        return wrap(x + dx, SIDE) * SIDE + wrap(y + dy, SIDE)
 
     def chunk(c):
         stage_d(c)
@@ -219,7 +228,7 @@
             out = jnp.dot(tokens_t[rows, :], acts[...], preferred_element_type=jnp.float32)
             return out.astype(jnp.bfloat16)
 
-        @pl.loop(1, N_DOM)
+        @pl.loop(0, N_DOM - 1)
         def _(k):
             t = target(k)
             grads[c, t] = block_of(t)
@@ -260,44 +269,55 @@
 
     pl.loop(0, CHUNKS)(products)
 
-    ar1[me] = part[...]
+    group = lax.broadcasted_iota(jnp.int32, (8, LANES), 1) // 32
+    packed = jnp.zeros((8, LANES), jnp.float32)
+    sums = part[...].reshape(2 * N_DOM, LANES)
+    for q in range(4):
+        own = sums[8 * q : 8 * q + 8]
+        own = own + pltpu.roll(own, 64, 1)
+        own = own + pltpu.roll(own, 32, 1)
+        packed = jnp.where(group == q, own, packed)
+    msg[...] = packed
+    ar1[me] = packed
 
     @pl.loop(1, N_DOM)
     def _(k):
         t = lax.rem(me + k, N_DOM)
-        remote(part, ar1.at[me], a1_s.at[t], a1_r.at[me], dom=t).start()
+        remote(msg, ar1.at[me], a1_s.at[t], a1_r.at[me], dom=t).start()
 
     @pl.loop(1, N_DOM)
     def _(k):
         t = lax.rem(me + k, N_DOM)
-        remote(part, ar1.at[t], a1_s.at[t], a1_r.at[t], dom=t).wait_recv()
+        remote(msg, ar1.at[t], a1_s.at[t], a1_r.at[t], dom=t).wait_recv()
 
     total = ar1[0]
     for j in range(1, N_DOM):
         total += ar1[j]
-    part2[...] = total
+    msg2[...] = total
     ar2[f] = total
 
     @pl.loop(1, N_FSDP)
     def _(k):
         t = lax.rem(f + k, N_FSDP)
-        remote(part2, ar2.at[f], a2_s.at[t], a2_r.at[f], fsdp=t).start()
+        remote(msg2, ar2.at[f], a2_s.at[t], a2_r.at[f], fsdp=t).start()
 
     @pl.loop(1, N_FSDP)
     def _(k):
         t = lax.rem(f + k, N_FSDP)
-        remote(part2, ar2.at[t], a2_s.at[t], a2_r.at[t], fsdp=t).wait_recv()
+        remote(msg2, ar2.at[t], a2_s.at[t], a2_r.at[t], fsdp=t).wait_recv()
 
     total = ar2[0]
     for j in range(1, N_FSDP):
         total += ar2[j]
-    total = jnp.sum(total.reshape(2 * N_DOM, LANES), axis=1, keepdims=True)
-    toward, own = total[:N_DOM], total[N_DOM:]
+    total = [jnp.sum(jnp.where(group == q, total, 0.0), axis=1, keepdims=True) for q in range(4)]
+    toward, own = jnp.concatenate(total[:2], axis=0), jnp.concatenate(total[2:], axis=0)
     spread = jnp.sum(prior * toward, axis=0, keepdims=True)
     cosine = toward / jnp.sqrt((own + EPS) * (spread + EPS))
     scaled = prior * jnp.exp(STEP_SIZE * cosine)
     alpha = scaled / jnp.sum(scaled, axis=0, keepdims=True)
-    oa_ref[...] = jnp.broadcast_to(alpha, (N_DOM, LANES))
+    row = lax.broadcasted_iota(jnp.int32, (N_DOM, N_DOM), 0)
+    lane = lax.broadcasted_iota(jnp.int32, (N_DOM, N_DOM), 1)
+    oa_ref[...] = jnp.sum(jnp.where(row == lane, alpha, 0.0), axis=0, keepdims=True)
     spread_out(alpha)
 
     for c in range(CHUNKS):
@@ -312,7 +332,7 @@
             og_ref[at, cols] = mix[:, :LANES]
             ou_ref[at, cols] = mix[:, LANES:]
 
-    for h in range(2):
+    for h in range(PIECES):
         for s in range(7):
             ring(s, h).wait_send()
         for s in range(8):
@@ -333,9 +353,9 @@
     @pl.loop(1, N_DOM)
     def _(k):
         t = lax.rem(me + k, N_DOM)
-        remote(part, ar1.at[me], a1_s.at[t], a1_r.at[me], dom=t).wait_send()
+        remote(msg, ar1.at[me], a1_s.at[t], a1_r.at[me], dom=t).wait_send()
         t = lax.rem(f + k, N_FSDP)
-        remote(part2, ar2.at[f], a2_s.at[t], a2_r.at[f], fsdp=t).wait_send()
+        remote(msg2, ar2.at[f], a2_s.at[t], a2_r.at[f], fsdp=t).wait_send()
 
 
 def local(tokens, hidden_grad, gate_weight, up_weight, counts):
@@ -347,9 +367,9 @@
         out_shape=(
             jax.ShapeDtypeStruct((ROWS, CHUNKS * LANES), f32),
             jax.ShapeDtypeStruct((ROWS, CHUNKS * LANES), f32),
-            jax.ShapeDtypeStruct((N_DOM, LANES), f32),
+            jax.ShapeDtypeStruct((1, N_DOM), f32),
         ),
-        in_specs=[vmem] * 5,
+        in_specs=[vmem] * 4 + [pl.BlockSpec(memory_space=pltpu.SMEM)],
         out_specs=(vmem,) * 3,
         scratch_shapes=[
             pltpu.VMEM((TOKENS, D), bf16),
@@ -361,10 +381,11 @@
             pltpu.VMEM((ROWS, 2 * LANES), f32),
             pltpu.VMEM((N_DOM, 1, 2 * LANES), f32),
             pltpu.VMEM((2 * N_DOM, 1, LANES), f32),
-            pltpu.VMEM((2 * N_DOM, 1, LANES), f32),
-            pltpu.VMEM((N_DOM, 2 * N_DOM, 1, LANES), f32),
-            pltpu.VMEM((N_FSDP, 2 * N_DOM, 1, LANES), f32),
-            dma((7, 2)), dma((7, 2)), dma((8, 2)), dma((8, 2)),
+            pltpu.VMEM((8, LANES), f32),
+            pltpu.VMEM((8, LANES), f32),
+            pltpu.VMEM((N_DOM, 8, LANES), f32),
+            pltpu.VMEM((N_FSDP, 8, LANES), f32),
+            dma((7, PIECES)), dma((7, PIECES)), dma((8, PIECES)), dma((8, PIECES)),
             dma((2, CHUNKS, 4)), dma((2, CHUNKS, 4)), dma((2, CHUNKS, 4)), dma((2, CHUNKS, 4)),
             dma((CHUNKS, N_DOM)), dma((CHUNKS, N_DOM)),
             dma((N_DOM,)), dma((N_DOM,)), dma((N_FSDP,)), dma((N_FSDP,)),
@@ -373,8 +394,8 @@
             collective_id=0, has_side_effects=True, vmem_limit_bytes=56 * 2**20
         ),
         cost_estimate=pl.CostEstimate(flops=13 * 10**9, bytes_accessed=4 * 10**6, transcendentals=400000),
-    )(tokens, hidden_grad, gate_weight, up_weight, counts.reshape(N_DOM, 1))
-    return mix_gate, mix_up, alpha[:, 0]
+    )(tokens, hidden_grad, gate_weight, up_weight, counts)
+    return mix_gate, mix_up, alpha.reshape(N_DOM)
 
 
 def solution(mesh):

time: 192 us -> 181 us (0.943)
  Pallas kernels: 186 us -> 177 us
  local copies, waits for them, and re-layouts: 5.37 us -> 3.24 us
    pallas_call x1, Pallas kernels: 186 us -> 177 us  [local(): pl.pallas_call(kernel, out_shape=(jax.ShapeDtypeStruct((ROWS, CHUNKS * LA...]
where the time goes in v2:
time: 181 us
  Pallas kernels  177 us (98%)
  local copies, waits for them, and re-layouts  3.24 us (2%)
    pallas_call x1, Pallas kernels, local(): pl.pallas_call(kernel, out_shape=(jax.ShapeDtypeStruct((ROWS, CHUNKS * LA...  177 us

profile of v2, /device:TPU:1, one launch (start us, length us, event | category | flops | bytes accessed | tf_op | source)
XLA Modules:
  0.0 180.9 jit_solution(17667687749082519549)
XLA Ops:
  0.6 177.0 %shard_map.76 = (f32[256,512]{1,0:T(8,128)}, f32[256,512]{1,0:T(8,128)}, f32[1,16]{1,0:T(1,128)}) custom-call(bf16[1,48,4096]{2,1,0:T(8,128)(2,1)} %tok_ref.1, bf16[1,768,512]{2,1,0:T(8,128)(2,1)} %hg_ref.1, bf16[256,512]{1,0:T(8,128)(2,1)} %gw_ref.1, bf16[256,512]{1,0:T(8,128)(2,1)} %uw_ref.1, s32[16]{0:T(128)} %cnt_ref.1), custom_call_target="tpu_custom_call" | custom-call | flops 12999999488 | bytes 4000000 | tf_op jit(solution)/shard_map/pallas_call | solution.py:365
  177.7 0.0 copy-start
  177.7 1.9 %copy.11 = f32[256,512]{1,0:T(8,128)} copy(f32[256,512]{1,0:T(8,128)} %get-tuple-element.12) | data formatting | bytes 1048576
  179.6 0.0 copy-done
  179.6 0.0 copy-start.1
  179.6 0.8 copy.12
  180.4 0.0 copy-done.1
  180.4 0.5 copy.13
Async XLA Ops:
  177.7 1.9 %copy-start = (f32[256,512]{1,0:T(8,128)S(1)}, f32[256,512]{1,0:T(8,128)}, u32[]{:S(2)}) copy-start(f32[256,512]{1,0:T(8,128)} %get-tuple-element.13) | copy-start | bytes 1572868
  179.6 0.8 copy-start.1

commit v3 on v2

--- a/solution.py
+++ b/solution.py
@@ -20,7 +20,7 @@
 TOK = 48
 TOKENS = 768
 D = 4096
-PIECES = 4
+PIECES = 2
 PIECE = D // PIECES
 ORDER = (10, 5, 15, 7, 13, 6, 14, 9, 11, 8, 2, 4, 1, 12, 3)
 
@@ -48,34 +48,45 @@
     way = 1 - 2 * core
     sibling = f + way
     onward = wrap(z + way, 8) * 2 + core
+    behind = wrap(z - way, 8) * 2 + core
 
     barrier = pltpu.get_barrier_semaphore()
 
-    @pl.loop(1, N_DOM)
-    def _(k):
-        pl.semaphore_signal(barrier, inc=1, device_id={"dom": lax.rem(me + k, N_DOM)}, device_id_type=MESH)
-        pl.semaphore_signal(barrier, inc=1, device_id={"fsdp": lax.rem(f + k, N_FSDP)}, device_id_type=MESH)
-
-    pl.semaphore_wait(barrier, 2 * (N_DOM - 1))
+    for where in (
+        {"dom": wrap(x + 1, SIDE) * SIDE + y},
+        {"dom": wrap(x - 1, SIDE) * SIDE + y},
+        {"dom": x * SIDE + wrap(y + 1, SIDE)},
+        {"dom": x * SIDE + wrap(y - 1, SIDE)},
+        {"fsdp": onward},
+        {"fsdp": behind},
+        {"fsdp": sibling},
+    ):
+        pl.semaphore_signal(barrier, inc=1, device_id=where, device_id_type=MESH)
+    pl.semaphore_wait(barrier, 7)
 
     def shard(s, c, h):
         owner = wrap(z - s * (1 - 2 * c) + 8, 8) * 2 + c
         return tokens.at[pl.ds(pl.multiple_of(owner * TOK, 16), TOK), pl.ds(h * PIECE, PIECE)]
 
-    def ring(s, h):
+    def ring(s, h, back=0):
         src = tok_ref.at[0, :, pl.ds(h * PIECE, PIECE)] if s == 0 else shard(s, core, h)
-        return remote(src, shard(s, core, h), rs_s.at[s, h], rs_r.at[s, h], fsdp=onward)
+        to = (onward, behind)[back]
+        i = 4 - s if back else s
+        return remote(src, shard(s, core, h), rs_s.at[i, h], rs_r.at[i, h], fsdp=to)
 
     def side(s, h):
         src = tok_ref.at[0, :, pl.ds(h * PIECE, PIECE)] if s == 0 else shard(s, core, h)
-        return remote(src, shard(s, core, h), sb_s.at[s, h], sb_r.at[s, h], fsdp=sibling)
+        return remote(src, shard(s, core, h), sb_s.at[s + 3, h], sb_r.at[s + 3, h], fsdp=sibling)
 
     def token_step(s):
         for h in range(PIECES):
             here = shard(s, core, h)
-            remote(here, here, rs_s.at[s - 1, h], rs_r.at[s - 1, h], fsdp=onward).wait_recv()
-            if s < 7:
+            i = s - 1 if s > 0 else 3 - s
+            remote(here, here, rs_s.at[i, h], rs_r.at[i, h], fsdp=onward).wait_recv()
+            if 0 < s < 4:
                 ring(s, h).start()
+            if -3 < s < 0:
+                ring(s, h, 1).start()
             side(s, h).start()
 
     def block(kind, c, bx, by, lo=0, n=ROWS):
@@ -124,6 +135,7 @@
 
     for h in range(PIECES):
         ring(0, h).start()
+        ring(0, h, 1).start()
 
     @pl.loop(0, CHUNKS)
     def _(c):
@@ -176,30 +188,27 @@
             for i in range(2, 4):
                 w2_got(kind, c, i)
 
+    pl.loop(0, CHUNKS)(stage_a)
     token_step(1)
-    pl.loop(0, CHUNKS)(stage_a)
+    token_step(-1)
+    stage_b(0)
+    stage_b(1)
+    stage_b(2)
+    stage_b(3)
     token_step(2)
-    pl.loop(0, CHUNKS)(stage_b)
+    token_step(-2)
+    stage_c(0)
+    stage_c(1)
     token_step(3)
-    stage_c(0)
+    token_step(-3)
     token_step(4)
-    stage_c(1)
-    token_step(5)
     stage_c(2)
-    token_step(6)
-    token_step(7)
-    stage_c(3)
 
     @pl.loop(0, 8)
     def _(s):
         for h in range(PIECES):
-            here = shard(s, 1 - core, h)
+            here = shard(s - 3, 1 - core, h)
             remote(here, here, sb_s.at[s, h], sb_r.at[s, h], fsdp=sibling).wait_recv()
-
-    @pl.loop(0, D // 256)
-    def _(k):
-        at = pl.ds(pl.multiple_of(k * 256, 256), 256)
-        tokens_t[at, :] = tokens[:, at].T
 
     def target(k):
         t = ORDER[0]
@@ -209,7 +218,7 @@
         dx, dy = dx + core * (dy - dx), dy + core * (dx - dy)
         return wrap(x + dx, SIDE) * SIDE + wrap(y + dy, SIDE)
 
-    def chunk(c):
+    def activations(c):
         stage_d(c)
 
         @pl.loop(0, TOKENS // 256)
@@ -223,8 +232,11 @@
             acts[at, :LANES] = (g * up * s * (1.0 + gate * (1.0 - s))).astype(jnp.bfloat16)
             acts[at, LANES:] = (g * gate * s).astype(jnp.bfloat16)
 
+    def gradients(c, turn=False):
         def block_of(t):
             rows = pl.ds(pl.multiple_of(t * ROWS, ROWS), ROWS)
+            if turn:
+                tokens_t[rows, :] = tokens[:, rows].T
             out = jnp.dot(tokens_t[rows, :], acts[...], preferred_element_type=jnp.float32)
             return out.astype(jnp.bfloat16)
 
@@ -236,13 +248,36 @@
 
         stack[c, me] = block_of(me)
 
-    pl.loop(0, CHUNKS)(chunk)
+    def chunk(c):
+        activations(c)
+        gradients(c)
+
+    activations(0)
+    gradients(0, True)
+    stage_c(3)
+    pl.loop(1, CHUNKS)(chunk)
+
+    for h in range(PIECES):
+        for s in range(4):
+            ring(s, h).wait_send()
+        for s in range(3):
+            ring(-s, h, 1).wait_send()
+        for s in range(-3, 5):
+            side(s, h).wait_send()
+
+    @pl.loop(0, CHUNKS)
+    def _(c):
+        for kind in range(2):
+            for i in range(4):
+                w1(kind, c, i).wait_send()
+                w2(kind, c, i).wait_send()
 
     def products(c):
         @pl.loop(1, N_DOM)
         def _(k):
             j = lax.rem(me + k, N_DOM)
             here = stack.at[c, j]
+            remote(grads.at[c, j], here, g_s.at[c, j], g_r.at[c, j], dom=j).wait_send()
             remote(here, here, g_s.at[c, j], g_r.at[c, j], dom=j).wait_recv()
 
         @pl.loop(0, ROWS // 32)
@@ -309,6 +344,12 @@
     total = ar2[0]
     for j in range(1, N_FSDP):
         total += ar2[j]
+    for k in range(1, N_DOM):
+        t = lax.rem(me + k, N_DOM)
+        remote(msg, ar1.at[me], a1_s.at[t], a1_r.at[me], dom=t).wait_send()
+        t = lax.rem(f + k, N_FSDP)
+        remote(msg2, ar2.at[f], a2_s.at[t], a2_r.at[f], fsdp=t).wait_send()
+
     total = [jnp.sum(jnp.where(group == q, total, 0.0), axis=1, keepdims=True) for q in range(4)]
     toward, own = jnp.concatenate(total[:2], axis=0), jnp.concatenate(total[2:], axis=0)
     spread = jnp.sum(prior * toward, axis=0, keepdims=True)
@@ -331,31 +372,6 @@
                 mix += scale[j] * stack[c, j, at, :].astype(jnp.float32)
             og_ref[at, cols] = mix[:, :LANES]
             ou_ref[at, cols] = mix[:, LANES:]
-
-    for h in range(PIECES):
-        for s in range(7):
-            ring(s, h).wait_send()
-        for s in range(8):
-            side(s, h).wait_send()
-
-    @pl.loop(0, CHUNKS)
-    def _(c):
-        for kind in range(2):
-            for i in range(4):
-                w1(kind, c, i).wait_send()
-                w2(kind, c, i).wait_send()
-
-        @pl.loop(1, N_DOM)
-        def _(k):
-            t = lax.rem(me + k, N_DOM)
-            remote(grads.at[c, t], stack.at[c, me], g_s.at[c, t], g_r.at[c, me], dom=t).wait_send()
-
-    @pl.loop(1, N_DOM)
-    def _(k):
-        t = lax.rem(me + k, N_DOM)
-        remote(msg, ar1.at[me], a1_s.at[t], a1_r.at[me], dom=t).wait_send()
-        t = lax.rem(f + k, N_FSDP)
-        remote(msg2, ar2.at[f], a2_s.at[t], a2_r.at[f], fsdp=t).wait_send()
 
 
 def local(tokens, hidden_grad, gate_weight, up_weight, counts):

time: 181 us -> 173 us (0.956)
  Pallas kernels: 177 us -> 169 us
    pallas_call x1, Pallas kernels: 177 us -> 169 us  [local(): pl.pallas_call(kernel, out_shape=(jax.ShapeDtypeStruct((ROWS, CHUNKS * LA...]
where the time goes in v3:
time: 173 us; the launch traced here: 172 us
  Pallas kernels  169 us (98%)
  local copies, waits for them, and re-layouts  3.24 us (2%)
    pallas_call x1, Pallas kernels, local(): pl.pallas_call(kernel, out_shape=(jax.ShapeDtypeStruct((ROWS, CHUNKS * LA...  169 us

profile of v3, /device:TPU:1, one launch (start us, length us, event | category | flops | bytes accessed | tf_op | source)
XLA Modules:
  0.0 172.5 jit_solution(18112209379920652220)
XLA Ops:
  0.6 168.6 %shard_map.76 = (f32[256,512]{1,0:T(8,128)}, f32[256,512]{1,0:T(8,128)}, f32[1,16]{1,0:T(1,128)}) custom-call(bf16[1,48,4096]{2,1,0:T(8,128)(2,1)} %tok_ref.1, bf16[1,768,512]{2,1,0:T(8,128)(2,1)} %hg_ref.1, bf16[256,512]{1,0:T(8,128)(2,1)} %gw_ref.1, bf16[256,512]{1,0:T(8,128)(2,1)} %uw_ref.1, s32[16]{0:T(128)} %cnt_ref.1), custom_call_target="tpu_custom_call" | custom-call | flops 12999999488 | bytes 4000000 | tf_op jit(solution)/shard_map/pallas_call | solution.py:381
  169.2 0.0 copy-start
  169.2 1.9 %copy.11 = f32[256,512]{1,0:T(8,128)} copy(f32[256,512]{1,0:T(8,128)} %get-tuple-element.12) | data formatting | bytes 1048576
  171.2 0.0 copy-done
  171.2 0.0 copy-start.1
  171.2 0.8 copy.12
  172.0 0.0 copy-done.1
  172.0 0.5 copy.13
Async XLA Ops:
  169.2 1.9 %copy-start = (f32[256,512]{1,0:T(8,128)S(1)}, f32[256,512]{1,0:T(8,128)}, u32[]{:S(2)}) copy-start(f32[256,512]{1,0:T(8,128)} %get-tuple-element.13) | copy-start | bytes 1572868
  171.2 0.8 copy-start.1

commit v4 on v3

v4 whole, which is shorter than its diff:
```python
import functools

import jax
import jax.numpy as jnp
from jax import lax
from jax.experimental import pallas as pl
from jax.experimental.pallas import tpu as pltpu
from jax.sharding import PartitionSpec as P

STEP_SIZE = 4.0
EPS = 1e-06
MESH = pl.DeviceIdType.MESH

SIDE = 4
N_DOM = 16
N_FSDP = 16
SHARED = 2
CHUNKS = 2
LANES = 128
ROWS = 256
TOK = 48
TOKENS = 768
D = 4096
PIECES = 2
PIECE = D // PIECES
ORDER = (5, 3, 7, 4, 2, 6, 1)


def wrap(i, n):
    return lax.rem(i + n, n)


def remote(src, dst, ss, rs, **where):
    return pltpu.make_async_remote_copy(
        src_ref=src, dst_ref=dst, send_sem=ss, recv_sem=rs, device_id=where, device_id_type=MESH
    )


def kernel(
    tok_ref, hg_ref, gw_ref, uw_ref, cnt_ref,
    og_ref, ou_ref, oa_ref,
    hg, tokens, tokens_t, weights, grads, stack, acts, mean, scale, part, msg, msg2, ar1, ar2, mix_s, mix_r,
    rs_s, rs_r, sb_s, sb_r, sw_s, sw_r, h_s, h_r, w1_s, w1_r, w2_s, w2_r, g_s, g_r, a1_s, a1_r, a2_s, a2_r, m_s, m_r,
):
    me = lax.axis_index("dom")
    x, y = me // SIDE, lax.rem(me, SIDE)
    f = lax.axis_index("fsdp")
    z, core = f // 2, lax.rem(f, 2)
    way = 1 - 2 * core
    sibling = f + way
    onward = wrap(z + way, 8) * 2 + core
    behind = wrap(z - way, 8) * 2 + core
    anti = wrap(x + 2, SIDE) * SIDE + wrap(y + 2, SIDE)
    u, v = x + core * (y - x), y + core * (x - y)

    def at_uv(u_, v_):
        return u_ * (4 - 3 * core) + v_ * (1 + 3 * core)

    def near_u(off):
        return at_uv(wrap(u + off, SIDE), v)

    def near_v(off):
        return at_uv(u, wrap(v + off, SIDE))

    def toward_pair(c):
        return 1 - 2 * lax.rem(v + c, 2)

    def half(c, v_):
        return lax.rem((v_ + c) // 2, 2)

    def columns(c, h):
        return pl.ds(pl.multiple_of((2 * c + h) * LANES, LANES), LANES)

    barrier = pltpu.get_barrier_semaphore()
    for where in (
        {"dom": near_u(1)},
        {"dom": near_u(-1)},
        {"dom": near_v(1)},
        {"dom": near_v(-1)},
        {"dom": near_v(2)},
        {"dom": anti},
        {"fsdp": onward},
        {"fsdp": behind},
        {"fsdp": sibling},
    ):
        pl.semaphore_signal(barrier, inc=1, device_id=where, device_id_type=MESH)
    pl.semaphore_wait(barrier, 9)

    def shard(w, s, c, h):
        owner = wrap(z - s * (1 - 2 * c) + 8, 8) * 2 + c
        return tokens.at[w, pl.ds(pl.multiple_of(owner * TOK, 16), TOK), pl.ds(h * PIECE, PIECE)]

    def source(w, s, h):
        if w == 0 and s == 0:
            return tok_ref.at[0, :, pl.ds(h * PIECE, PIECE)]
        return shard(w, s, core, h)

    def ring(w, s, h, back=0):
        i = 4 - s if back else s
        return remote(
            source(w, s, h), shard(w, s, core, h), rs_s.at[w, i, h], rs_r.at[w, i, h], fsdp=(onward, behind)[back]
        )

    def side(w, s, h):
        return remote(source(w, s, h), shard(w, s, core, h), sb_s.at[w, s + 3, h], sb_r.at[w, s + 3, h], fsdp=sibling)

    def token_start(w):
        for h in range(PIECES):
            ring(w, 0, h).start()
            ring(w, 0, h, 1).start()

    def token_step(w, s):
        for h in range(PIECES):
            here = shard(w, s, core, h)
            i = s - 1 if s > 0 else 3 - s
            remote(here, here, rs_s.at[w, i, h], rs_r.at[w, i, h], fsdp=onward).wait_recv()
            if 0 < s < 4:
                ring(w, s, h).start()
            if -3 < s < 0:
                ring(w, s, h, 1).start()
            side(w, s, h).start()

    def token_side(w):
        @pl.loop(0, 8)
        def _(s):
            for h in range(PIECES):
                here = shard(w, s - 3, 1 - core, h)
                remote(here, here, sb_s.at[w, s, h], sb_r.at[w, s, h], fsdp=sibling).wait_recv()

    own_rows = pl.ds(pl.multiple_of(f * TOK, 16), TOK)

    def swap():
        return remote(tok_ref.at[0], tokens.at[1, own_rows], sw_s.at[0], sw_r.at[0], dom=anti)

    def swap_hg(c):
        return remote(hg_ref.at[0, :, columns(c, 1 - half(c, v))], hg.at[1, c], h_s.at[c], h_r.at[c], dom=anti)

    def w1(c, kind, o):
        to = wrap(v + o, SIDE)
        src = (gw_ref, uw_ref)[kind].at[:, columns(c, half(c, to))]
        return remote(src, weights.at[c, kind, x, y], w1_s.at[c, kind, o], w1_r.at[c, kind, o], dom=at_uv(u, to))

    def w1_got(c, kind, o):
        d = near_v(-o)
        here = weights.at[c, kind, d // SIDE, lax.rem(d, SIDE)]
        remote(here, here, w1_s.at[c, kind, o], w1_r.at[c, kind, o], dom=d).wait_recv()

    MID = ROWS // 2

    def line(axis, c, off, lo=0, n=ROWS):
        at = wrap(u + off, SIDE)
        if axis == 0:
            return weights.at[c, :, at, :, pl.ds(lo, n)]
        return weights.at[c, :, :, at, pl.ds(lo, n)]

    def w2(axis, c, i):
        to = (1, -1)[i % 2]
        src = line(axis, c, 0) if i < 2 else line(axis, c, -to, (i - 2) * MID, MID)
        return remote(src, src, w2_s.at[c, i], w2_r.at[c, i], dom=near_u(to))

    def w2_got(axis, c, i):
        to = (1, -1)[i % 2]
        here = line(axis, c, -to) if i < 2 else line(axis, c, 2, (i - 2) * MID, MID)
        remote(here, here, w2_s.at[c, i], w2_r.at[c, i], dom=near_u(to)).wait_recv()

    def by_core(do):
        for axis in range(2):
            pl.when(core == axis)(functools.partial(do, axis))

    def stage_b(axis):
        for c in range(CHUNKS):
            for i in range(2):
                w2(axis, c, i).start()

    def stage_c(c, axis):
        for i in range(2):
            w2_got(axis, c, i)
            w2(axis, c, i + 2).start()

    def stage_d(c, axis):
        for i in range(2, 4):
            w2_got(axis, c, i)

    token_start(0)
    swap().start()
    for c in range(CHUNKS):
        for kind in range(2):
            for o in (2, 1, 3):
                w1(c, kind, o).start()
    for h in range(PIECES):
        side(0, 0, h).start()

    tokens[0, own_rows, :] = tok_ref[0]
    for c in range(CHUNKS):
        cols = columns(c, half(c, v))
        weights[c, 0, x, y] = gw_ref[:, cols]
        weights[c, 1, x, y] = uw_ref[:, cols]
        hg[0, c] = hg_ref[0, :, cols]

    def spread_out(column):
        for j in range(N_DOM):
            scale[j] = jnp.broadcast_to(column[j : j + 1, :], (1, 2 * LANES))

    count = cnt_ref[0]
    for j in range(1, N_DOM):
        count += cnt_ref[j]
    count = jnp.full((1, 2 * LANES), count.astype(jnp.float32))
    for j in range(N_DOM):
        scale[j] = jnp.full((1, 2 * LANES), cnt_ref[j].astype(jnp.float32)) / count
    prior = scale[...].reshape(N_DOM, 2 * LANES)[:, :1]
    part[...] = jnp.zeros_like(part)

    for c in range(CHUNKS):
        for kind in range(2):
            for o in (2, 1, 3):
                w1_got(c, kind, o)
    by_core(stage_b)
    for c in range(CHUNKS):
        swap_hg(c).start()
    token_step(0, 1)
    token_step(0, -1)
    by_core(functools.partial(stage_c, 0))
    token_step(0, 2)
    token_step(0, -2)
    by_core(functools.partial(stage_c, 1))
    remote(tokens.at[1, own_rows], tokens.at[1, own_rows], sw_s.at[0], sw_r.at[0], dom=anti).wait_recv()
    token_step(0, 3)
    token_step(0, -3)
    token_start(1)
    for h in range(PIECES):
        side(1, 0, h).start()
    token_step(0, 4)
    token_side(0)
    by_core(functools.partial(stage_d, 0))

    def activations(w, c):
        @pl.loop(0, TOKENS // 256)
        def _(m):
            at = pl.ds(pl.multiple_of(m * 256, 256), 256)
            wide = jnp.concatenate([weights[c, 0].reshape(D, LANES), weights[c, 1].reshape(D, LANES)], axis=1)
            pre = jnp.dot(tokens[w, at, :], wide, preferred_element_type=jnp.float32)
            gate, up = pre[:, :LANES], pre[:, LANES:]
            g = hg[w, c, at, :].astype(jnp.float32)
            s = jax.nn.sigmoid(gate)
            acts[at, :LANES] = (g * up * s * (1.0 + gate * (1.0 - s))).astype(jnp.bfloat16)
            acts[at, LANES:] = (g * gate * s).astype(jnp.bfloat16)

    def gradients(w, c, turn):
        way_v = toward_pair(c)
        domain = (me, anti)[w]

        def block_of(d):
            rows = pl.ds(pl.multiple_of(d * ROWS, ROWS), ROWS)
            if turn:
                tokens_t[w, rows, :] = tokens[w, :, rows].T
            out = jnp.dot(tokens_t[w, rows, :], acts[...], preferred_element_type=jnp.float32)
            return out.astype(jnp.bfloat16)

        @pl.loop(0, 7)
        def _(k):
            i = ORDER[0]
            for n in range(1, 7):
                i = jnp.where(k == n, ORDER[n], i)
            du, pair = i // 2, lax.rem(i, 2)
            u_ = wrap(u + du, SIDE)
            first = wrap(v + pair * way_v, SIDE)
            grads[w, c, i, :ROWS, :] = block_of(at_uv(u_, first))
            grads[w, c, i, ROWS:, :] = block_of(at_uv(u_, wrap(v - way_v + 3 * pair * way_v + 4, SIDE)))
            remote(
                grads.at[w, c, i], stack.at[c, domain], g_s.at[w, c, i], g_r.at[w, c, i], dom=at_uv(u_, first)
            ).start()

        stack[c, domain, :ROWS, :] = block_of(me)
        stack[c, domain, ROWS:, :] = block_of(near_v(-way_v))

    activations(0, 0)
    gradients(0, 0, True)
    token_step(1, 1)
    token_step(1, -1)
    by_core(functools.partial(stage_d, 1))
    activations(0, 1)
    token_step(1, 2)
    token_step(1, -2)
    gradients(0, 1, False)
    token_step(1, 3)
    token_step(1, -3)
    token_step(1, 4)
    for c in range(CHUNKS):
        remote(hg.at[1, c], hg.at[1, c], h_s.at[c], h_r.at[c], dom=anti).wait_recv()
    token_side(1)
    activations(1, 0)
    gradients(1, 0, True)
    activations(1, 1)
    gradients(1, 1, False)

    for w in range(SHARED):
        for h in range(PIECES):
            for s in range(4):
                ring(w, s, h).wait_send()
            for s in range(3):
                ring(w, -s, h, 1).wait_send()
            for s in range(-3, 5):
                side(w, s, h).wait_send()
    swap().wait_send()
    for c in range(CHUNKS):
        swap_hg(c).wait_send()
        for kind in range(2):
            for o in (2, 1, 3):
                w1(c, kind, o).wait_send()

    def stage_e(axis):
        for c in range(CHUNKS):
            for i in range(4):
                w2(axis, c, i).wait_send()

    by_core(stage_e)

    def products(c):
        way_v = toward_pair(c)
        for w in range(SHARED):

            @pl.loop(1, 8)
            def _(i):
                u_, v_ = wrap(u - i // 2, SIDE), wrap(v + lax.rem(i, 2) * way_v, SIDE)
                if w == 0:
                    domain = at_uv(u_, v_)
                else:
                    domain = at_uv(wrap(u_ + 2, SIDE), wrap(v_ + 2, SIDE))
                here = stack.at[c, domain]
                remote(grads.at[w, c, i], here, g_s.at[w, c, i], g_r.at[w, c, i], dom=at_uv(u_, v_)).wait_send()
                remote(here, here, g_s.at[w, c, i], g_r.at[w, c, i], dom=at_uv(u_, v_)).wait_recv()

        @pl.loop(0, 2 * ROWS // 32)
        def _(r):
            at = pl.ds(pl.multiple_of(r * 32, 32), 32)
            total = scale[0] * stack[c, 0, at, :].astype(jnp.float32)
            for j in range(1, N_DOM):
                total += scale[j] * stack[c, j, at, :].astype(jnp.float32)
            mean[at, :] = total

        @pl.loop(0, N_DOM)
        def _(j):
            toward = jnp.zeros((8, 2 * LANES), jnp.float32)
            own = jnp.zeros((8, 2 * LANES), jnp.float32)
            for r in range(2 * ROWS // 32):
                at = pl.ds(r * 32, 32)
                g = stack[c, j, at, :].astype(jnp.float32)
                toward += jnp.sum((g * mean[at, :]).reshape(4, 8, 2 * LANES), axis=0)
                own += jnp.sum((g * g).reshape(4, 8, 2 * LANES), axis=0)
            toward = jnp.sum(toward, axis=0, keepdims=True)
            own = jnp.sum(own, axis=0, keepdims=True)
            part[j] += toward[:, :LANES] + toward[:, LANES:]
            part[N_DOM + j] += own[:, :LANES] + own[:, LANES:]

    for c in range(CHUNKS):
        products(c)

    group = lax.broadcasted_iota(jnp.int32, (8, LANES), 1) // 32
    packed = jnp.zeros((8, LANES), jnp.float32)
    sums = part[...].reshape(2 * N_DOM, LANES)
    for q in range(4):
        own = sums[8 * q : 8 * q + 8]
        own = own + pltpu.roll(own, 64, 1)
        own = own + pltpu.roll(own, 32, 1)
        packed = jnp.where(group == q, own, packed)
    msg[...] = packed
    ar1[me] = packed

    @pl.loop(1, N_DOM)
    def _(k):
        t = lax.rem(me + k, N_DOM)
        remote(msg, ar1.at[me], a1_s.at[t], a1_r.at[me], dom=t).start()

    @pl.loop(1, N_DOM)
    def _(k):
        t = lax.rem(me + k, N_DOM)
        remote(msg, ar1.at[t], a1_s.at[t], a1_r.at[t], dom=t).wait_recv()

    total = ar1[0]
    for j in range(1, N_DOM):
        total += ar1[j]
    msg2[...] = total
    ar2[f] = total

    @pl.loop(1, N_FSDP)
    def _(k):
        t = lax.rem(f + k, N_FSDP)
        remote(msg2, ar2.at[f], a2_s.at[t], a2_r.at[f], fsdp=t).start()

    @pl.loop(1, N_FSDP)
    def _(k):
        t = lax.rem(f + k, N_FSDP)
        remote(msg2, ar2.at[t], a2_s.at[t], a2_r.at[t], fsdp=t).wait_recv()

    total = ar2[0]
    for j in range(1, N_FSDP):
        total += ar2[j]
    for k in range(1, N_DOM):
        t = lax.rem(me + k, N_DOM)
        remote(msg, ar1.at[me], a1_s.at[t], a1_r.at[me], dom=t).wait_send()
        t = lax.rem(f + k, N_FSDP)
        remote(msg2, ar2.at[f], a2_s.at[t], a2_r.at[f], fsdp=t).wait_send()

    total = [jnp.sum(jnp.where(group == q, total, 0.0), axis=1, keepdims=True) for q in range(4)]
    toward, own = jnp.concatenate(total[:2], axis=0), jnp.concatenate(total[2:], axis=0)
    spread = jnp.sum(prior * toward, axis=0, keepdims=True)
    cosine = toward / jnp.sqrt((own + EPS) * (spread + EPS))
    scaled = prior * jnp.exp(STEP_SIZE * cosine)
    alpha = scaled / jnp.sum(scaled, axis=0, keepdims=True)
    row = lax.broadcasted_iota(jnp.int32, (N_DOM, N_DOM), 0)
    lane = lax.broadcasted_iota(jnp.int32, (N_DOM, N_DOM), 1)
    oa_ref[...] = jnp.sum(jnp.where(row == lane, alpha, 0.0), axis=0, keepdims=True)
    spread_out(alpha)

    def mixed(c, lo, r):
        at = pl.ds(pl.multiple_of(lo + r * 32, 32), 32)
        mix = scale[0] * stack[c, 0, at, :].astype(jnp.float32)
        for j in range(1, N_DOM):
            mix += scale[j] * stack[c, j, at, :].astype(jnp.float32)
        return mix

    def over(c):
        return remote(mix_s.at[c], mix_r.at[c], m_s.at[c], m_r.at[c], dom=near_v(-toward_pair(c)))

    for c in range(CHUNKS):

        @pl.loop(0, ROWS // 32)
        def _(r):
            mix_s[c, pl.ds(pl.multiple_of(r * 32, 32), 32), :] = mixed(c, ROWS, r)

        over(c).start()

    for c in range(CHUNKS):
        cols = columns(c, half(c, v))

        @pl.loop(0, ROWS // 32)
        def _(r):
            at = pl.ds(pl.multiple_of(r * 32, 32), 32)
            mix = mixed(c, 0, r)
            og_ref[at, cols] = mix[:, :LANES]
            ou_ref[at, cols] = mix[:, LANES:]

    for c in range(CHUNKS):
        cols = columns(c, 1 - half(c, v))
        over(c).wait_recv()
        og_ref[:, cols] = mix_r[c, :, :LANES]
        ou_ref[:, cols] = mix_r[c, :, LANES:]
    for c in range(CHUNKS):
        over(c).wait_send()


def local(tokens, hidden_grad, gate_weight, up_weight, counts):
    vmem = pl.BlockSpec(memory_space=pltpu.VMEM)
    dma = pltpu.SemaphoreType.DMA
    bf16, f32 = jnp.bfloat16, jnp.float32
    mix_gate, mix_up, alpha = pl.pallas_call(
        kernel,
        out_shape=(
            jax.ShapeDtypeStruct((ROWS, 4 * LANES), f32),
            jax.ShapeDtypeStruct((ROWS, 4 * LANES), f32),
            jax.ShapeDtypeStruct((1, N_DOM), f32),
        ),
        in_specs=[vmem] * 4 + [pl.BlockSpec(memory_space=pltpu.SMEM)],
        out_specs=(vmem,) * 3,
        scratch_shapes=[
            pltpu.VMEM((SHARED, CHUNKS, TOKENS, LANES), bf16),
            pltpu.VMEM((SHARED, TOKENS, D), bf16),
            pltpu.VMEM((SHARED, D, TOKENS), bf16),
            pltpu.VMEM((CHUNKS, 2, SIDE, SIDE, ROWS, LANES), bf16),
            pltpu.VMEM((SHARED, CHUNKS, 8, 2 * ROWS, 2 * LANES), bf16),
            pltpu.VMEM((CHUNKS, N_DOM, 2 * ROWS, 2 * LANES), bf16),
            pltpu.VMEM((TOKENS, 2 * LANES), bf16),
            pltpu.VMEM((2 * ROWS, 2 * LANES), f32),
            pltpu.VMEM((N_DOM, 1, 2 * LANES), f32),
            pltpu.VMEM((2 * N_DOM, 1, LANES), f32),
            pltpu.VMEM((8, LANES), f32),
            pltpu.VMEM((8, LANES), f32),
            pltpu.VMEM((N_DOM, 8, LANES), f32),
            pltpu.VMEM((N_FSDP, 8, LANES), f32),
            pltpu.VMEM((CHUNKS, ROWS, 2 * LANES), f32),
            pltpu.VMEM((CHUNKS, ROWS, 2 * LANES), f32),
            dma((SHARED, 7, PIECES)), dma((SHARED, 7, PIECES)), dma((SHARED, 8, PIECES)), dma((SHARED, 8, PIECES)),
            dma((1,)), dma((1,)), dma((CHUNKS,)), dma((CHUNKS,)),
            dma((CHUNKS, 2, 4)), dma((CHUNKS, 2, 4)), dma((CHUNKS, 4)), dma((CHUNKS, 4)),
            dma((SHARED, CHUNKS, 8)), dma((SHARED, CHUNKS, 8)),
            dma((N_DOM,)), dma((N_DOM,)), dma((N_FSDP,)), dma((N_FSDP,)), dma((CHUNKS,)), dma((CHUNKS,)),
        ],
        compiler_params=pltpu.CompilerParams(
            collective_id=0, has_side_effects=True, vmem_limit_bytes=60 * 2**20
        ),
        cost_estimate=pl.CostEstimate(flops=13 * 10**9, bytes_accessed=4 * 10**6, transcendentals=400000),
    )(tokens, hidden_grad, gate_weight, up_weight, counts)
    return mix_gate, mix_up, alpha.reshape(N_DOM)


def solution(mesh):
    return jax.shard_map(
        local,
        mesh=mesh,
        in_specs=(
            P("dom", "fsdp", None),
            P("dom", None, "fsdp"),
            P("dom", "fsdp"),
            P("dom", "fsdp"),
            P(),
        ),
        out_specs=(P("dom", "fsdp"), P("dom", "fsdp"), P()),
        check_vma=False,
    )
```

time: 173 us -> 167 us (0.965)
  Pallas kernels: 169 us -> 163 us
    pallas_call x1, Pallas kernels: 169 us -> 163 us  [local(): pl.pallas_call(kernel, out_shape=(jax.ShapeDtypeStruct((ROWS, 4 * LANES),...]
where the time goes in v4:
time: 167 us
  Pallas kernels  163 us (98%)
  local copies, waits for them, and re-layouts  3.24 us (2%)
    pallas_call x1, Pallas kernels, local(): pl.pallas_call(kernel, out_shape=(jax.ShapeDtypeStruct((ROWS, 4 * LANES),...  163 us

profile of v4, /device:TPU:1, one launch (start us, length us, event | category | flops | bytes accessed | tf_op | source)
XLA Modules:
  0.0 167.2 jit_solution(11487856117705274212)
XLA Ops:
  0.6 163.3 %shard_map.76 = (f32[256,512]{1,0:T(8,128)}, f32[256,512]{1,0:T(8,128)}, f32[1,16]{1,0:T(1,128)}) custom-call(bf16[1,48,4096]{2,1,0:T(8,128)(2,1)} %tok_ref.1, bf16[1,768,512]{2,1,0:T(8,128)(2,1)} %hg_ref.1, bf16[256,512]{1,0:T(8,128)(2,1)} %gw_ref.1, bf16[256,512]{1,0:T(8,128)(2,1)} %uw_ref.1, s32[16]{0:T(128)} %cnt_ref.1), custom_call_target="tpu_custom_call" | custom-call | flops 12999999488 | bytes 4000000 | tf_op jit(solution)/shard_map/pallas_call | solution.py:456
  164.0 0.0 copy-start
  164.0 1.9 %copy.11 = f32[256,512]{1,0:T(8,128)} copy(f32[256,512]{1,0:T(8,128)} %get-tuple-element.12) | data formatting | bytes 1048576
  165.9 0.0 copy-done
  165.9 0.0 copy-start.1
  165.9 0.8 copy.12
  166.7 0.0 copy-done.1
  166.7 0.5 copy.13
Async XLA Ops:
  164.0 1.9 %copy-start = (f32[256,512]{1,0:T(8,128)S(1)}, f32[256,512]{1,0:T(8,128)}, u32[]{:S(2)}) copy-start(f32[256,512]{1,0:T(8,128)} %get-tuple-element.13) | copy-start | bytes 1572868
  165.9 0.8 copy-start.1

commit v5 on v4

--- a/solution.py
+++ b/solution.py
@@ -167,10 +167,9 @@
         for axis in range(2):
             pl.when(core == axis)(functools.partial(do, axis))
 
-    def stage_b(axis):
-        for c in range(CHUNKS):
-            for i in range(2):
-                w2(axis, c, i).start()
+    def stage_b(c, axis):
+        for i in range(2):
+            w2(axis, c, i).start()
 
     def stage_c(c, axis):
         for i in range(2):
@@ -214,22 +213,22 @@
         for kind in range(2):
             for o in (2, 1, 3):
                 w1_got(c, kind, o)
-    by_core(stage_b)
+        by_core(functools.partial(stage_b, c))
     for c in range(CHUNKS):
         swap_hg(c).start()
     token_step(0, 1)
     token_step(0, -1)
-    by_core(functools.partial(stage_c, 0))
     token_step(0, 2)
     token_step(0, -2)
-    by_core(functools.partial(stage_c, 1))
-    remote(tokens.at[1, own_rows], tokens.at[1, own_rows], sw_s.at[0], sw_r.at[0], dom=anti).wait_recv()
+    by_core(functools.partial(stage_c, 0))
     token_step(0, 3)
     token_step(0, -3)
+    by_core(functools.partial(stage_c, 1))
+    token_step(0, 4)
+    remote(tokens.at[1, own_rows], tokens.at[1, own_rows], sw_s.at[0], sw_r.at[0], dom=anti).wait_recv()
     token_start(1)
     for h in range(PIECES):
         side(1, 0, h).start()
-    token_step(0, 4)
     token_side(0)
     by_core(functools.partial(stage_d, 0))
 

time: 167 us -> 162 us (0.970)
  Pallas kernels: 163 us -> 158 us
    pallas_call x1, Pallas kernels: 163 us -> 158 us  [local(): pl.pallas_call(kernel, out_shape=(jax.ShapeDtypeStruct((ROWS, 4 * LANES),...]
where the time goes in v5:
time: 162 us
  Pallas kernels  158 us (98%)
  local copies, waits for them, and re-layouts  3.24 us (2%)
    pallas_call x1, Pallas kernels, local(): pl.pallas_call(kernel, out_shape=(jax.ShapeDtypeStruct((ROWS, 4 * LANES),...  158 us

profile of v5, /device:TPU:1, one launch (start us, length us, event | category | flops | bytes accessed | tf_op | source)
XLA Modules:
  0.0 161.7 jit_solution(14549533576611024982)
XLA Ops:
  0.6 157.8 %shard_map.76 = (f32[256,512]{1,0:T(8,128)}, f32[256,512]{1,0:T(8,128)}, f32[1,16]{1,0:T(1,128)}) custom-call(bf16[1,48,4096]{2,1,0:T(8,128)(2,1)} %tok_ref.1, bf16[1,768,512]{2,1,0:T(8,128)(2,1)} %hg_ref.1, bf16[256,512]{1,0:T(8,128)(2,1)} %gw_ref.1, bf16[256,512]{1,0:T(8,128)(2,1)} %uw_ref.1, s32[16]{0:T(128)} %cnt_ref.1), custom_call_target="tpu_custom_call" | custom-call | flops 12999999488 | bytes 4000000 | tf_op jit(solution)/shard_map/pallas_call | solution.py:455
  158.4 0.0 copy-start
  158.4 1.9 %copy.11 = f32[256,512]{1,0:T(8,128)} copy(f32[256,512]{1,0:T(8,128)} %get-tuple-element.12) | data formatting | bytes 1048576
  160.4 0.0 copy-done
  160.4 0.0 copy-start.1
  160.4 0.8 copy.12
  161.2 0.0 copy-done.1
  161.2 0.5 copy.13
Async XLA Ops:
  158.4 1.9 %copy-start = (f32[256,512]{1,0:T(8,128)S(1)}, f32[256,512]{1,0:T(8,128)}, u32[]{:S(2)}) copy-start(f32[256,512]{1,0:T(8,128)} %get-tuple-element.13) | copy-start | bytes 1572868
  160.4 0.8 copy-start.1

commit v6 on v5

--- a/solution.py
+++ b/solution.py
@@ -278,9 +278,9 @@
     token_step(1, -1)
     by_core(functools.partial(stage_d, 1))
     activations(0, 1)
+    gradients(0, 1, False)
     token_step(1, 2)
     token_step(1, -2)
-    gradients(0, 1, False)
     token_step(1, 3)
     token_step(1, -3)
     token_step(1, 4)

time: 162 us -> 161 us (level)
  no operation moved by 1% of the time
where the time goes in v6:
time: 161 us
  Pallas kernels  157 us (98%)
  local copies, waits for them, and re-layouts  3.24 us (2%)
    pallas_call x1, Pallas kernels, local(): pl.pallas_call(kernel, out_shape=(jax.ShapeDtypeStruct((ROWS, 4 * LANES),...  157 us
    unnamed x7, local copies, waits for them, and re-layouts  3.24 us

profile of v6, /device:TPU:1, one launch (start us, length us, event | category | flops | bytes accessed | tf_op | source)
XLA Modules:
  0.0 160.6 jit_solution(4566620845609595986)
XLA Ops:
  0.6 156.7 %shard_map.76 = (f32[256,512]{1,0:T(8,128)}, f32[256,512]{1,0:T(8,128)}, f32[1,16]{1,0:T(1,128)}) custom-call(bf16[1,48,4096]{2,1,0:T(8,128)(2,1)} %tok_ref.1, bf16[1,768,512]{2,1,0:T(8,128)(2,1)} %hg_ref.1, bf16[256,512]{1,0:T(8,128)(2,1)} %gw_ref.1, bf16[256,512]{1,0:T(8,128)(2,1)} %uw_ref.1, s32[16]{0:T(128)} %cnt_ref.1), custom_call_target="tpu_custom_call" | custom-call | flops 12999999488 | bytes 4000000 | tf_op jit(solution)/shard_map/pallas_call | solution.py:455
  157.4 0.0 copy-start
  157.4 1.9 %copy.11 = f32[256,512]{1,0:T(8,128)} copy(f32[256,512]{1,0:T(8,128)} %get-tuple-element.12) | data formatting | bytes 1048576
  159.3 0.0 copy-done
  159.3 0.0 copy-start.1
  159.3 0.8 copy.12
  160.1 0.0 copy-done.1
  160.1 0.5 copy.13
Async XLA Ops:
  157.4 1.9 %copy-start = (f32[256,512]{1,0:T(8,128)S(1)}, f32[256,512]{1,0:T(8,128)}, u32[]{:S(2)}) copy-start(f32[256,512]{1,0:T(8,128)} %get-tuple-element.13) | copy-start | bytes 1572868
  159.3 0.8 copy-start.1
